TPU v7x, 256 devices: a whole 4x4x8 slice. The times are simulated.
256 devices in a mesh: dp: 32 (over y, z_hi, core), tensor: 8 (over z_lo, x).
Axes of the slice: x: 4, y: 4, z: 8 (z_hi: 4, z_lo: 2; z = z_hi * 2 + z_lo), core: 2. Of those that a mesh axis runs over, the one named last changes fastest.
Arguments:
- cotangent: bfloat16 [32768, 4096], P(('dp', 'tensor')), may hold values from -24 to 24
- features: bfloat16 [32768, 1024], P(('dp', 'tensor')), may hold values from -24 to 24
- normed: bfloat16 [32768, 1024], P(('dp', 'tensor')), may hold values from -24 to 24
- pre_hidden: bfloat16 [32768, 4096], P('dp', 'tensor'), may hold values from -6 to 6
- pre_inner: bfloat16 [32768, 4096], P('dp', 'tensor'), may hold values from -8 to 8
- w_first: bfloat16 [1024, 4096], P(None, 'tensor'), may hold values from -0.1875 to 0.1875
- w_second: bfloat16 [4096, 4096], P('tensor'), may hold values from -0.09375 to 0.09375
- w_down: bfloat16 [4096, 1024], P('tensor'), may hold values from -0.09375 to 0.09375
Outputs:
- grad_second: float32 [4096, 4096], P('tensor', 'dp')
- grad_first: float32 [1024, 4096], P('dp', 'tensor')
- grad_down: float32 [4096, 1024], P('tensor', 'dp')
- grad_up: float32 [1024, 4096], P('dp', 'tensor')
- encoder_cotangent: bfloat16 [32768, 1024], P(('dp', 'tensor'))
All inputs are finite; a program needn't handle non-finite values.
Results may differ from a plain program's by a relative error of at most 0.02.
Values may be sent and summed in bfloat16 or wider, within the bound.
A program may use at most 128 MiB of HBM per device.

v0:
```python
import math

import jax
import jax.numpy as jnp
from jax import lax
from jax.sharding import PartitionSpec as P


def normal_cdf(value):
    return 0.5 * (1.0 + jax.scipy.special.erf(value * (1.0 / math.sqrt(2.0))))


def normal_pdf(value):
    return jnp.exp(-0.5 * value * value) * (1.0 / math.sqrt(2.0 * math.pi))


def over_rows(left, right):
    return lax.dot_general(
        left, right, (((0,), (0,)), ((), ())), preferred_element_type=jnp.float32
    )


def over_cols(left, right):
    return lax.dot_general(
        left, right, (((1,), (1,)), ((), ())), preferred_element_type=jnp.float32
    )


def on_device(cotangent, features, normed, pre_hidden, pre_inner, w_first, w_second, w_down):
    tok_rows = cotangent.shape[0]
    tensor_count = lax.axis_size("tensor")
    replica_count = lax.axis_size("dp")
    factor = 1.0 / math.sqrt(tok_rows * tensor_count * replica_count)
    pre_value = pre_hidden.astype(jnp.float32)
    hidden_act = (pre_value * normal_cdf(pre_value)).astype(jnp.bfloat16)
    slope = normal_cdf(pre_value) + pre_value * normal_pdf(pre_value)
    piece = lax.all_gather(cotangent, "tensor", axis=0, tiled=True)
    accum = over_rows(hidden_act, piece)
    d_hidden = over_cols(piece, w_second)
    accum, d_hidden = (accum, d_hidden)
    grad_second = lax.psum_scatter(accum * factor, "dp", scatter_dimension=1, tiled=True)
    d_pre = (d_hidden * slope).astype(jnp.bfloat16)
    feat_all, norm_all = (
        lax.all_gather(features, "tensor", axis=0, tiled=True),
        lax.all_gather(normed, "tensor", axis=0, tiled=True),
    )
    first_term = over_rows(feat_all, d_pre) * factor
    own_rows = lax.psum_scatter(
        over_cols(d_pre, w_first).astype(jnp.bfloat16), "tensor", scatter_dimension=0, tiled=True
    )
    cot_all = lax.all_gather(own_rows, "tensor", axis=0, tiled=True)
    inner_value = pre_inner.astype(jnp.float32)
    sig = jax.nn.sigmoid(1.702 * inner_value)
    inner_act = (inner_value * sig).astype(jnp.bfloat16)
    down_term = over_rows(cot_all, inner_act) * factor
    d_act = over_cols(cot_all, w_down)
    d_inner = (d_act * (sig + 1.702 * inner_value * sig * (1.0 - sig))).astype(jnp.bfloat16)
    up_term = over_rows(norm_all, d_inner) * factor
    grad_first, grad_up, down_rows = (
        lax.psum_scatter(first_term, "dp", scatter_dimension=0, tiled=True),
        lax.psum_scatter(up_term, "dp", scatter_dimension=0, tiled=True),
        lax.psum_scatter(down_term, "dp", scatter_dimension=0, tiled=True),
    )
    return (grad_second, grad_first, down_rows.T, grad_up, own_rows)


def solution(mesh):
    return jax.shard_map(
        on_device,
        mesh=mesh,
        in_specs=(
            P(("dp", "tensor"), None),
            P(("dp", "tensor"), None),
            P(("dp", "tensor"), None),
            P("dp", "tensor"),
            P("dp", "tensor"),
            P(None, "tensor"),
            P("tensor", None),
            P("tensor", None),
        ),
        out_specs=(
            P("tensor", "dp"),
            P("dp", "tensor"),
            P("tensor", "dp"),
            P("dp", "tensor"),
            P(("dp", "tensor"), None),
        ),
        check_vma=False,
    )
```

profile of v0, /device:TPU:1, one launch (start us, length us, event | category | flops | bytes accessed | tf_op | source)
XLA Modules:
  0.0 712.6 jit_solution(7468318923826055815)
XLA Ops:
  7.2 0.0 copy-start
  7.2 0.0 all-gather.5.cloned.1.call-start
  7.2 0.7 all-gather.5.cloned.1.call-update
  7.9 0.0 reduce-scatter.12.cloned.1.call-start
  8.0 100.2 %all-gather.5.cloned.1.call-done = bf16[1024,4096]{1,0:T(8,128)(2,1)} async-done(((bf16[128,4096]{1,0:T(8,128)(2,1)}), bf16[1024,4096]{1,0:T(8,128)(2,1)}) %all-gather.5.cloned.1.call-update) | async-done | bytes 8388624 | tf_op jit(solution)/shard_map/all_gather | solution.py:37
  108.1 10.0 %fusion.18 = bf16[1024,512]{1,0:T(8,128)(2,1)S(1)} fusion(bf16[1024,512]{1,0:T(8,128)(2,1)} %param.11, bf16[1024,4096]{1,0:T(8,128)(2,1)} %all-gather.5.cloned.1.call-done, bf16[512,4096]{1,0:T(8,128)(2,1)} %param.14), kind=kOutput, calls=%fused_computation.26 | convolution fusion | flops 4300734464 | bytes 14680064 | tf_op jit(solution)/shard_map/dot_general | solution.py:24
  118.1 0.0 copy-start.2
  118.1 1.0 copy-done.2
  119.1 0.0 copy-done
  119.1 2.7 convolution_convert_fusion
  121.8 0.0 reduce-scatter.12.cloned.1.call-update
  121.8 0.0 all-gather.7.cloned.1.call-start
  121.8 0.7 all-gather.7.cloned.1.call-update
  122.5 0.0 all-gather.9.cloned.1.call-start
  122.6 38.1 %reduce-scatter.12.cloned.1.call-done = bf16[128,1024]{1,0:T(8,128)(2,1)} async-done(((bf16[1024,1024]{1,0:T(8,128)(2,1)}), bf16[128,1024]{1,0:T(8,128)(2,1)}) %reduce-scatter.12.cloned.1.call-update) | async-done | bytes 262160 | tf_op jit(solution)/shard_map/reduce_scatter | solution.py:48
  160.7 0.0 all-gather.9.cloned.1.call-update
  160.7 0.0 all-gather.11.cloned.1.call-start
  160.8 0.5 all-gather.11.cloned.1.call-update
  161.3 0.0 reduce-scatter.16.cloned.1.call-start
  161.3 44.5 %all-gather.7.cloned.1.call-done = bf16[1024,1024]{1,0:T(8,128)(2,1)} async-done(((bf16[128,1024]{1,0:T(8,128)(2,1)}), bf16[1024,1024]{1,0:T(8,128)(2,1)}) %all-gather.7.cloned.1.call-update) | async-done | bytes 2097168 | tf_op jit(solution)/shard_map/all_gather | solution.py:44
  205.9 3.2 multiply_bitcast_fusion.1
  209.1 1.8 copy.17
  210.9 0.0 copy-start.3
  210.9 0.0 reduce-scatter.16.cloned.1.call-update
  210.9 0.0 reduce-scatter.14.cloned.1.call-start
  211.0 40.5 %all-gather.9.cloned.1.call-done = bf16[1024,1024]{1,0:T(8,128)(2,1)} async-done(((bf16[128,1024]{1,0:T(8,128)(2,1)}), bf16[1024,1024]{1,0:T(8,128)(2,1)}) %all-gather.9.cloned.1.call-update) | async-done | bytes 2097168 | tf_op jit(solution)/shard_map/all_gather | solution.py:51
  251.5 0.0 copy-done.3
  251.5 4.3 convolution_multiply_fusion.1
  255.8 0.0 reduce-scatter.14.cloned.1.call-update
  255.8 0.0 reduce-scatter.18.cloned.1.call-start
  255.9 40.6 %all-gather.11.cloned.1.call-done = bf16[1024,1024]{1,0:T(8,128)(2,1)} async-done(((bf16[128,1024]{1,0:T(8,128)(2,1)}), bf16[1024,1024]{1,0:T(8,128)(2,1)}) %all-gather.11.cloned.1.call-update) | async-done | bytes 2097168 | tf_op jit(solution)/shard_map/all_gather | solution.py:45
  296.5 5.7 multiply_bitcast_fusion
  302.2 1.9 copy.19
  304.1 0.0 copy-start.1
  304.1 0.0 reduce-scatter.18.cloned.1.call-update
  304.1 0.2 reduce-scatter.10.cloned.1.call-start
  304.3 1.0 copy-done.1
  305.3 10.4 %convolution_multiply_fusion = f32[512,4096]{1,0:T(8,128)} fusion(bf16[1024,4096]{1,0:T(8,128)(2,1)} %all-gather.5.cloned.1.call-done, bf16[1024,512]{1,0:T(8,128)(2,1)S(1)} %copy-done.1), kind=kOutput, calls=%fused_computation | convolution fusion | flops 4300210176 | bytes 17825792 | tf_op jit(solution)/shard_map/dot_general | solution.py:18
  315.7 0.0 reduce-scatter.10.cloned.1.call-update
  315.7 78.7 %reduce-scatter.16.cloned.1.call-done = f32[32,512]{1,0:T(8,128)} async-done(((f32[1024,512]{1,0:T(8,128)}), f32[32,512]{1,0:T(8,128)}) %reduce-scatter.16.cloned.1.call-update) | async-done | bytes 65552
  394.4 93.5 %reduce-scatter.14.cloned.1.call-done = f32[32,512]{1,0:T(8,128)} async-done(((f32[1024,512]{1,0:T(8,128)}), f32[32,512]{1,0:T(8,128)}) %reduce-scatter.14.cloned.1.call-update) | async-done | bytes 65552 | tf_op jit(solution)/shard_map/reduce_scatter | solution.py:62
  488.0 93.6 %reduce-scatter.18.cloned.1.call-done = f32[32,512]{1,0:T(8,128)} async-done(((f32[1024,512]{1,0:T(8,128)}), f32[32,512]{1,0:T(8,128)}) %reduce-scatter.18.cloned.1.call-update) | async-done | bytes 65552
  581.6 124.5 %reduce-scatter.10.cloned.1.call-done = f32[512,128]{1,0:T(8,128)} async-done(((f32[512,4096]{1,0:T(8,128)}), f32[512,128]{1,0:T(8,128)}) %reduce-scatter.10.cloned.1.call-update) | async-done | bytes 262160 | tf_op jit(solution)/shard_map/reduce_scatter | solution.py:41
Async XLA Ops:
  7.2 111.9 %copy-start = (bf16[1024,512]{1,0:T(8,128)(2,1)S(1)}, bf16[1024,512]{1,0:T(8,128)(2,1)}, u32[]{:S(2)}) copy-start(bf16[1024,512]{1,0:T(8,128)(2,1)} %param.13) | copy-start | bytes 3145732
  7.2 101.0 %all-gather.5.cloned.1.call-start = ((), (), s32[]{:S(2)}) async-start(), calls=%async_computation.5 | async-start | bytes 9437184 | tf_op jit(solution)/shard_map/all_gather | solution.py:37
  7.9 152.8 %reduce-scatter.12.cloned.1.call-start = ((), (), s32[]{:S(2)}) async-start(), calls=%async_computation.8 | async-start | bytes 2359296 | tf_op jit(solution)/shard_map/reduce_scatter | solution.py:48
  118.1 1.0 copy-start.2
  121.8 84.1 %all-gather.7.cloned.1.call-start = ((), (), s32[]{:S(2)}) async-start(), calls=%async_computation.7 | async-start | bytes 2359296 | tf_op jit(solution)/shard_map/all_gather | solution.py:44
  122.5 129.0 %all-gather.9.cloned.1.call-start = ((), (), s32[]{:S(2)}) async-start(), calls=%async_computation.9 | async-start | bytes 2359296 | tf_op jit(solution)/shard_map/all_gather | solution.py:51
  160.7 135.8 %all-gather.11.cloned.1.call-start = ((), (), s32[]{:S(2)}) async-start(), calls=%async_computation.11 | async-start | bytes 2359296 | tf_op jit(solution)/shard_map/all_gather | solution.py:45
  161.3 233.1 %reduce-scatter.16.cloned.1.call-start = ((), (), s32[]{:S(2)}) async-start(), calls=%async_computation.12 | async-start | bytes 2162688
  210.9 40.6 %copy-start.3 = (bf16[1024,512]{1,0:T(8,128)(2,1)S(1)}, bf16[1024,512]{1,0:T(8,128)(2,1)}, u32[]{:S(2)}) copy-start(bf16[1024,512]{1,0:T(8,128)(2,1)} %param.12) | copy-start | bytes 3145732
  210.9 277.0 %reduce-scatter.14.cloned.1.call-start = ((), (), s32[]{:S(2)}) async-start(), calls=%async_computation.10 | async-start | bytes 2162688 | tf_op jit(solution)/shard_map/reduce_scatter | solution.py:62
  255.8 325.8 %reduce-scatter.18.cloned.1.call-start = ((), (), s32[]{:S(2)}) async-start(), calls=%async_computation.13 | async-start | bytes 2162688
  304.1 1.2 copy-start.1
  304.1 402.0 %reduce-scatter.10.cloned.1.call-start = ((), (), s32[]{:S(2)}) async-start(), calls=%async_computation.6 | async-start | bytes 8650752 | tf_op jit(solution)/shard_map/reduce_scatter | solution.py:41
Sparse Core Ops, SparseCore 0:
  9.8 98.2 all-gather.4
  121.9 38.7 reduce-scatter.11
  162.5 43.3 all-gather.6
  208.1 43.3 all-gather.8
  253.1 43.3 all-gather.10
  300.8 93.6 reduce-scatter.15
  398.9 89.0 reduce-scatter.13
  492.4 89.1 reduce-scatter.17
  586.2 119.8 reduce-scatter.9
where the time goes:
time: 713 us
  waiting for transfers between devices  656 us (92%)
  matrix products  36.2 us (5%)
  between operations  13.9 us (2%)
    unnamed x11, waiting for transfers between devices  174 us
    reduce_scatter x1, waiting for transfers between devices, on_device(): lax.psum_scatter(accum * factor, 'dp', scatter_dimension=1, tiled=True)  125 us
    all_gather x1, waiting for transfers between devices, on_device(): piece = lax.all_gather(cotangent, 'tensor', axis=0, tiled=True)  100 us
    reduce_scatter x1, waiting for transfers between devices, on_device(): lax.psum_scatter(down_term, 'dp', scatter_dimension=0, tiled=True)  93.5 us
    all_gather x1, waiting for transfers between devices, on_device(): lax.all_gather(features, 'tensor', axis=0, tiled=True)  44.5 us
    all_gather x1, waiting for transfers between devices, on_device(): lax.all_gather(normed, 'tensor', axis=0, tiled=True)  40.6 us
    all_gather x1, waiting for transfers between devices, on_device(): cot_all = lax.all_gather(own_rows, 'tensor', axis=0, tiled=True)  40.5 us
    reduce_scatter x1, waiting for transfers between devices, on_device(): lax.psum_scatter(over_cols(d_pre, w_first).astype(jnp.bfloat16), 'tensor'...  38.1 us
  transfers between devices with their start and end apart: 9, of which 9 were waited for; matrix products, arithmetic and copies ran while one was open for 4% of the time, Pallas kernels for 0%

commit v1 on v0

v1 whole, which is shorter than its diff:
```python
import math

import jax
import jax.numpy as jnp
from jax import lax
from jax.experimental import pallas as pl
from jax.experimental.pallas import tpu as pltpu
from jax.sharding import PartitionSpec as P

MESH = pl.DeviceIdType.MESH
BF = jnp.bfloat16
F32 = jnp.float32
NX, NY, NZ = 4, 4, 8
K = 8
FEAT, NORM, ENC = K, K + 1, K + 2


def dot_nn(left, right):
    return lax.dot_general(left, right, (((1,), (0,)), ((), ())), preferred_element_type=F32)


def dot_nt(left, right):
    return lax.dot_general(left, right, (((1,), (1,)), ((), ())), preferred_element_type=F32)


def dot_tn(left, right):
    return lax.dot_general(left, right, (((0,), (0,)), ((), ())), preferred_element_type=F32)


def device(x, y, z, core):
    return {"dp": y * 8 + (z // 2) * 2 + core, "tensor": lax.rem(z, 2) * 4 + x}


def wait(ref, sem):
    pltpu.make_async_copy(ref, ref, sem).wait()


def send(src, dst, send_sem, recv_sem, to):
    pltpu.make_async_remote_copy(
        src_ref=src, dst_ref=dst, send_sem=send_sem, recv_sem=recv_sem, device_id=to, device_id_type=MESH
    ).start()


def kernel(
    cot_in, feat_in, norm_in, preh_in, prei_in, w1_in, w2_in, wd_in,
    o_gs, o_small, o_enc,
    cot, w2, w1, wd, preh, prei, feat, norm, hact_t, slope, dhid, dpre,
    encp, encc, encs, encr, enc, iact, dinner,
    gsp, gsr, gsy, gsz, smp, smr, smy, smz,
    ag_s, ag_r, cot_l, w2_l, fn_l,
    w2_s, w2_r, w_s, w1_r, wd_r, pre_s, pre_r,
    ec_s, ec_r, ex_s, ex_r,
    gy_s, gy_r, gz_s, gz_r, sy_s, sy_r, sz_s, sz_r,
):
    dp, tensor = lax.axis_index("dp"), lax.axis_index("tensor")
    y, zh, c = dp // 8, lax.rem(dp // 2, 4), lax.rem(dp, 2)
    a, x = tensor // 4, lax.rem(tensor, 4)
    z = 2 * zh + a
    home = a == c
    xp, xm, x2 = lax.rem(x + 1, NX), lax.rem(x + 3, NX), lax.rem(x + 2, NX)
    right, left, other = device(xp, y, z, c), device(xm, y, z, c), device(x, y, z, 1 - c)
    partner_z = z + 1 - 2 * a
    outer_z = lax.rem(z + 2 * a - 1 + NZ, NZ)
    partner, outer = device(x, y, partner_z, a), device(x, y, outer_z, a)
    mine = c * 4 + x

    def rows_of(ref, shard, start=0, size=128):
        return ref.at[pl.ds(pl.multiple_of(shard * 128 + start, 64), size)]

    def view(item):
        if isinstance(item, int) and item >= K:
            return {FEAT: feat, NORM: norm, ENC: enc}[item]
        return cot.at[item]

    pltpu.make_async_copy(feat_in, rows_of(feat, mine), fn_l.at[0]).start()
    pltpu.make_async_copy(norm_in, rows_of(norm, mine), fn_l.at[1]).start()

    @pl.loop(0, K)
    def _(k):
        for quarter in range(4):
            cols = pl.ds(pl.multiple_of(quarter * 1024 + ((k % 4) * 2 + k // 4) * 128, 128), 128)
            to = pl.ds(quarter * 128, 128)
            pltpu.make_async_copy(
                cot_in.at[:, cols],
                cot.at[k, pl.ds(pl.multiple_of(mine * 128, 128), 128), to],
                cot_l.at[k],
            ).start()
            pltpu.make_async_copy(w2_in.at[:, cols], w2.at[a, k, :, to], w2_l.at[k]).start()

    barrier = pltpu.get_barrier_semaphore()
    friends = [right, left, device(x2, y, z, c), other]
    friends += [device(x, lax.rem(y + o, NY), z, c) for o in (1, 2, 3)]
    friends += [device(x, y, lax.rem(z + o, NZ), core) for o in range(1, NZ) for core in (0, 1)]
    for friend in friends:
        pl.semaphore_signal(barrier, inc=1, device_id=friend, device_id_type=MESH)
    pl.semaphore_wait(barrier, len(friends))

    def gather_start(item):
        buf = view(item)
        own = rows_of(buf, mine)
        send(own, own, ag_s.at[item, 0], ag_r.at[item, 0], right)
        send(own, own, ag_s.at[item, 1], ag_r.at[item, 1], left)
        send(own, own, ag_s.at[item, 2], ag_r.at[item, 4], other)

    def gather_middle(item):
        buf = view(item)
        from_left, from_right = rows_of(buf, c * 4 + xm), rows_of(buf, c * 4 + xp)
        wait(from_left, ag_r.at[item, 0])
        half = rows_of(buf, c * 4 + xm, 0, 64)
        send(half, half, ag_s.at[item, 3], ag_r.at[item, 2], right)
        send(from_left, from_left, ag_s.at[item, 4], ag_r.at[item, 5], other)
        wait(from_right, ag_r.at[item, 1])
        half = rows_of(buf, c * 4 + xp, 64, 64)
        send(half, half, ag_s.at[item, 5], ag_r.at[item, 3], left)
        send(from_right, from_right, ag_s.at[item, 6], ag_r.at[item, 6], other)

    def gather_last(item):
        buf = view(item)
        far = rows_of(buf, c * 4 + x2)
        wait(rows_of(buf, c * 4 + x2, 0, 64), ag_r.at[item, 2])
        wait(rows_of(buf, c * 4 + x2, 64, 64), ag_r.at[item, 3])
        send(far, far, ag_s.at[item, 7], ag_r.at[item, 7], other)

    def gather_end(item):
        buf = view(item)
        for index, at in ((4, x), (5, xm), (6, xp), (7, x2)):
            wait(rows_of(buf, (1 - c) * 4 + at), ag_r.at[item, index])

    def gather_sent(item):
        buf = view(item)
        whole, half = rows_of(buf, mine), rows_of(buf, mine, 0, 64)
        for index in range(8):
            wait(half if index in (3, 5) else whole, ag_s.at[item, index])

    def weights_start(k):
        wait(w2.at[a, k], w2_l.at[k])
        for index, (start, to) in enumerate(((c * 128, outer), (256 + c * 128, partner))):
            piece = w2.at[a, k, pl.ds(pl.multiple_of(start, 128), 128)]
            send(piece, piece, w2_s.at[k, index], w2_r.at[k, 2 * index + c], to)

    def weights_end(k):
        @pl.when(jnp.logical_not(home))
        def _():
            for index in range(4):
                wait(w2.at[c, k, pl.ds(index * 128, 128)], w2_r.at[k, index])

    def chunk_start(k):
        wait(cot.at[k, pl.ds(pl.multiple_of(mine * 128, 128), 128)], cot_l.at[k])
        gather_start(k)
        weights_start(k)

    def halves_start(src, dst, size, sems, first, to):
        part = pl.ds(pl.multiple_of(c * size, size), size)
        send(src.at[part], dst.at[part], w_s.at[first], sems.at[c], to)

        @pl.when(home)
        def _():
            for index in range(2):
                rows = pl.ds(index * size, size)
                pltpu.make_async_copy(src.at[rows], dst.at[rows], sems.at[index]).start()

    def halves_end(dst, size, sems):
        for index in range(2):
            wait(dst.at[pl.ds(index * size, size)], sems.at[index])

    def pre_start(index, src, dst):
        to_rows = pl.ds(pl.multiple_of(c * 512, 512), 512)

        def part(low):
            return src.at[pl.ds(pl.multiple_of(low * 512, 512), 512)]

        send(part(1 - a), dst.at[to_rows], pre_s.at[index, 0], pre_r.at[index, c], partner)

        @pl.when(home)
        def _():
            pltpu.make_async_copy(part(a), dst.at[to_rows], pre_r.at[index, c]).start()

        @pl.when(jnp.logical_not(home))
        def _():
            send(part(a), dst.at[to_rows], pre_s.at[index, 1], pre_r.at[index, c], other)

    def pre_end(index, dst):
        for core in range(2):
            wait(dst.at[pl.ds(core * 512, 512)], pre_r.at[index, core])

    def hidden_parts():
        pre_end(0, preh)

        @pl.loop(0, 8)
        def _(r):
            rows = pl.ds(pl.multiple_of(r * 128, 128), 128)
            value = preh[rows, :].astype(F32)
            cdf = 0.5 * (1.0 + lax.erf(value * (1.0 / math.sqrt(2.0))))
            pdf = jnp.exp(-0.5 * value * value) * (1.0 / math.sqrt(2.0 * math.pi))
            slope[rows, :] = cdf + value * pdf
            hact_t[:, rows] = jnp.transpose(value * cdf).astype(BF)

    def inner_parts():
        pre_end(1, prei)

        @pl.loop(0, 8)
        def _(r):
            rows = pl.ds(pl.multiple_of(r * 128, 128), 128)
            value = prei[rows, :].astype(F32)
            sig = 1.0 / (1.0 + jnp.exp(-1.702 * value))
            iact[rows, :] = (value * sig).astype(BF)
            dhid[rows, :] = sig + 1.702 * value * sig * (1.0 - sig)

    def chunk_work(k):
        @pl.loop(0, 2)
        def _(r):
            rows = pl.ds(pl.multiple_of(r * 512, 512), 512)
            dhid[rows, :] += dot_nt(cot[k, rows, :], w2[c, k])

        for half in range(2):
            term = dot_nn(hact_t[...], cot[k, :, half * 256:(half + 1) * 256])
            gsp[k, 2 * half] = term[:, :128].astype(BF)
            gsp[k, 2 * half + 1] = term[:, 128:].astype(BF)
        for o in (1, 2, 3):
            to = lax.rem(y + o, NY)
            send(gsp.at[k, to], gsr.at[k, o - 1], gy_s.at[k, o - 1], gy_r.at[k, o - 1], device(x, to, z, c))

    def chunk_sum(k):
        for o in range(3):
            wait(gsr.at[k, o], gy_r.at[k, o])
        total = gsp[k, y].astype(F32)
        for o in range(3):
            total = total + gsr[k, o].astype(F32)
        gsy[k] = total.astype(BF)
        to_z, core = 2 * lax.rem(k, 4) + c, k // 4
        own = jnp.logical_and(to_z == z, core == c)

        @pl.when(own)
        def _():
            pltpu.make_async_copy(gsy.at[k], gsz.at[z], gz_r.at[z]).start()

        @pl.when(jnp.logical_not(own))
        def _():
            send(gsy.at[k], gsz.at[z], gz_s.at[k], gz_r.at[z], device(x, y, to_z, core))

    def chunk_sum_sent(k):
        own = jnp.logical_and(2 * lax.rem(k, 4) + c == z, k // 4 == c)

        @pl.when(jnp.logical_not(own))
        def _():
            wait(gsy.at[k], gz_s.at[k])

    def small_start(i):
        for o in (1, 2, 3):
            to = lax.rem(y + o, NY)
            send(
                smp.at[i, pl.ds(pl.multiple_of(to * 256, 256), 256)], smr.at[i, o - 1],
                sy_s.at[i, o - 1], sy_r.at[i, o - 1], device(x, to, z, c),
            )

    def small_piece(i, hi, core):
        return smy.at[i, pl.ds(hi * 64 + core * 32, 32)]

    def small_sum(i):
        for o in range(3):
            wait(smr.at[i, o], sy_r.at[i, o])
        total = smp[i, pl.ds(pl.multiple_of(y * 256, 256), 256), :].astype(F32)
        for o in range(3):
            total = total + smr[i, o].astype(F32)
        smy[i] = total.astype(BF)
        for hi in range(4):
            for core in range(2):
                to_z = 2 * hi + c
                own = jnp.logical_and(to_z == z, core == c)

                @pl.when(own)
                def _():
                    pltpu.make_async_copy(small_piece(i, hi, core), smz.at[i, z], sz_r.at[i, z]).start()

                @pl.when(jnp.logical_not(own))
                def _():
                    send(
                        small_piece(i, hi, core), smz.at[i, z],
                        sz_s.at[i, hi, core], sz_r.at[i, z], device(x, y, to_z, core),
                    )

    def small_end(i):
        total = jnp.zeros((32, 512), F32)
        for source in range(NZ):
            wait(smz.at[i, source], sz_r.at[i, source])
            total = total + smz[i, source].astype(F32)
        o_small[i] = total

    def small_sent(i):
        for o in range(3):
            wait(smr.at[i, o], sy_s.at[i, o])
        for hi in range(4):
            for core in range(2):
                own = jnp.logical_and(2 * hi + c == z, core == c)

                @pl.when(jnp.logical_not(own))
                def _():
                    wait(small_piece(i, hi, core), sz_s.at[i, hi, core])

    def row_product(i, left, right):
        for part in range(2):
            cols = slice(part * 512, (part + 1) * 512)
            smp[i, cols, :] = dot_tn(left[:, cols], right[...]).astype(BF)

    pre_start(0, preh_in, preh)
    chunk_start(0)
    chunk_start(1)
    dhid[...] = jnp.zeros_like(dhid)

    @pl.loop(0, K + 2)
    def _(t):
        @pl.when(t + 2 < K)
        def _():
            chunk_start(t + 2)

        @pl.when(t == 5)
        def _():
            halves_start(w1_in, w1, 512, w1_r, 0, outer)
            pre_start(1, prei_in, prei)

        @pl.when(t == 6)
        def _():
            halves_start(wd_in, wd, 256, wd_r, 1, outer)
            wait(rows_of(feat, mine), fn_l.at[0])
            gather_start(FEAT)

        @pl.when(t < K)
        def _():
            gather_middle(t)

        @pl.when(jnp.logical_and(t >= 1, t <= K))
        def _():
            gather_last(t - 1)

        @pl.when(t == 2)
        def _():
            hidden_parts()

        @pl.when(t >= 4)
        def _():
            chunk_sum(t - 4)

        @pl.when(t >= 2)
        def _():
            gather_end(t - 2)
            weights_end(t - 2)
            chunk_work(t - 2)

    @pl.loop(0, 4)
    def _(r):
        rows = pl.ds(pl.multiple_of(r * 256, 256), 256)
        dpre[rows, :] = (dhid[rows, :] * slope[rows, :]).astype(BF)

    halves_end(w1, 512, w1_r)

    def partials(core):
        for pair in range(2):
            rows = pl.ds(pl.multiple_of(core * 512 + pair * 256, 256), 256)
            term = dot_nt(dpre[rows, :], w1[...]).astype(BF)
            encp[core, 2 * pair] = term[:128]
            encp[core, 2 * pair + 1] = term[128:]

    partials(1 - c)
    for at in range(4):
        send(encp.at[1 - c, at], encc.at[at], ec_s.at[at], ec_r.at[at], other)
    gather_middle(FEAT)
    partials(c)
    for at in range(4):
        wait(encc.at[at], ec_r.at[at])
    for o in (2, 1, 3):
        to = lax.rem(x + o, NX)
        encs[o - 1] = (encp[c, to].astype(F32) + encc[to].astype(F32)).astype(BF)
        send(encs.at[o - 1], encr.at[o - 1], ex_s.at[o - 1], ex_r.at[o - 1], device(to, y, z, c))
    wait(rows_of(norm, mine), fn_l.at[1])
    gather_start(NORM)
    gather_last(FEAT)
    chunk_sum(K - 2)
    chunk_sum(K - 1)
    gather_end(FEAT)
    row_product(0, feat, dpre)
    small_start(0)
    inner_parts()
    total = encp[c, x].astype(F32) + encc[x].astype(F32)
    for o in range(3):
        wait(encr.at[o], ex_r.at[o])
        total = total + encr[o].astype(F32)
    own_rows = total.astype(BF)
    enc[pl.ds(pl.multiple_of(mine * 128, 128), 128), :] = own_rows
    o_enc[...] = own_rows
    gather_start(ENC)
    gather_middle(NORM)
    gather_middle(ENC)
    gather_last(ENC)
    gather_last(NORM)
    small_sum(0)
    gather_end(ENC)
    row_product(1, enc, iact)
    small_start(1)
    halves_end(wd, 256, wd_r)

    @pl.loop(0, 4)
    def _(r):
        rows = pl.ds(pl.multiple_of(r * 256, 256), 256)
        dinner[rows, :] = (dot_nt(enc[rows, :], wd[...]) * dhid[rows, :]).astype(BF)

    gather_end(NORM)
    row_product(2, norm, dinner)
    small_start(2)

    total = jnp.zeros((512, 128), F32)
    for source in range(NZ):
        wait(gsz.at[source], gz_r.at[source])
        total = total + gsz[source].astype(F32)
    o_gs[...] = total
    small_end(0)
    small_sum(1)
    small_sum(2)
    small_end(1)
    small_end(2)

    @pl.loop(0, K)
    def _(k):
        gather_sent(k)
        for index in range(2):
            wait(w2.at[a, k, pl.ds(0, 128)], w2_s.at[k, index])
        for o in range(3):
            wait(gsr.at[k, o], gy_s.at[k, o])
        chunk_sum_sent(k)

    for item in (FEAT, NORM, ENC):
        gather_sent(item)
    wait(w1.at[pl.ds(0, 512)], w_s.at[0])
    wait(wd.at[pl.ds(0, 256)], w_s.at[1])
    for index in range(2):
        wait(preh.at[pl.ds(0, 512)], pre_s.at[index, 0])

        @pl.when(jnp.logical_not(home))
        def _():
            wait(preh.at[pl.ds(0, 512)], pre_s.at[index, 1])

    for at in range(4):
        wait(encc.at[at], ec_s.at[at])
    for o in range(3):
        wait(encr.at[o], ex_s.at[o])
    for i in range(3):
        small_sent(i)


def on_device(cotangent, features, normed, pre_hidden, pre_inner, w_first, w_second, w_down):
    tok_rows = cotangent.shape[0]
    factor = 1.0 / math.sqrt(tok_rows * lax.axis_size("tensor") * lax.axis_size("dp"))
    dma = pltpu.SemaphoreType.DMA
    vmem = pltpu.VMEM
    gs, small, own_rows = pl.pallas_call(
        kernel,
        out_shape=(
            jax.ShapeDtypeStruct((512, 128), F32),
            jax.ShapeDtypeStruct((3, 32, 512), F32),
            jax.ShapeDtypeStruct((128, 1024), BF),
        ),
        in_specs=[pl.BlockSpec(memory_space=pl.ANY)] * 8,
        out_specs=(pl.BlockSpec(memory_space=pltpu.VMEM),) * 3,
        scratch_shapes=[
            vmem((K, 1024, 512), BF),
            vmem((2, K, 512, 512), BF),
            vmem((1024, 512), BF),
            vmem((512, 1024), BF),
            vmem((1024, 512), BF),
            vmem((1024, 512), BF),
            vmem((1024, 1024), BF),
            vmem((1024, 1024), BF),
            vmem((512, 1024), BF),
            vmem((1024, 512), F32),
            vmem((1024, 512), F32),
            vmem((1024, 512), BF),
            vmem((2, 4, 128, 1024), BF),
            vmem((4, 128, 1024), BF),
            vmem((3, 128, 1024), BF),
            vmem((3, 128, 1024), BF),
            vmem((1024, 1024), BF),
            vmem((1024, 512), BF),
            vmem((1024, 512), BF),
            vmem((K, 4, 512, 128), BF),
            vmem((K, 3, 512, 128), BF),
            vmem((K, 512, 128), BF),
            vmem((NZ, 512, 128), BF),
            vmem((3, 1024, 512), BF),
            vmem((3, 3, 256, 512), BF),
            vmem((3, 256, 512), BF),
            vmem((3, NZ, 32, 512), BF),
            dma((K + 3, 8)), dma((K + 3, 8)), dma((K,)), dma((K,)), dma((2,)),
            dma((K, 2)), dma((K, 4)), dma((2,)), dma((2,)), dma((2,)), dma((2, 2)), dma((2, 2)),
            dma((4,)), dma((4,)), dma((3,)), dma((3,)),
            dma((K, 3)), dma((K, 3)), dma((K,)), dma((NZ,)),
            dma((3, 3)), dma((3, 3)), dma((3, 4, 2)), dma((3, NZ)),
        ],
        compiler_params=pltpu.CompilerParams(
            collective_id=0, has_side_effects=True, vmem_limit_bytes=63 * 2**20
        ),
        name="backward",
    )(cotangent, features, normed, pre_hidden, pre_inner, w_first, w_second, w_down)
    gs, small = gs * factor, small * factor
    return (gs, small[0], small[1].T, small[2], own_rows)


def solution(mesh):
    return jax.shard_map(
        on_device,
        mesh=mesh,
        in_specs=(
            P(("dp", "tensor"), None),
            P(("dp", "tensor"), None),
            P(("dp", "tensor"), None),
            P("dp", "tensor"),
            P("dp", "tensor"),
            P(None, "tensor"),
            P("tensor", None),
            P("tensor", None),
        ),
        out_specs=(
            P("tensor", "dp"),
            P("dp", "tensor"),
            P("tensor", "dp"),
            P("dp", "tensor"),
            P(("dp", "tensor"), None),
        ),
        check_vma=False,
    )
```

time: 713 us -> 148 us (0.21)
  waiting for transfers between devices: 656 us -> 0 us
  Pallas kernels: 0 us -> 143 us
  matrix products: 36.2 us -> 0 us
  between operations: 13.9 us -> 0.65 us
    reduce_scatter x3 -> x0, waiting for transfers between devices: 256 us -> none  [the longest x1 125 us: on_device(): lax.psum_scatter(accum * factor, 'dp', scatter_dimension=1, tiled=True)]
    all_gather x4 -> x0, waiting for transfers between devices: 226 us -> none  [the longest x1 100 us: on_device(): piece = lax.all_gather(cotangent, 'tensor', axis=0, tiled=True)]
    unnamed x11 -> x0, waiting for transfers between devices: 174 us -> none
    pallas_call x0 -> x1, Pallas kernels: none -> 143 us  [on_device(): pl.pallas_call(kernel, out_shape=(jax.ShapeDtypeStruct((512, 128), F32),...]
    dot_general x6 -> x0, matrix products: 36.2 us -> none  [the longest x4 23.6 us: over_rows(): lax.dot_general(left, right, (((0,), (0,)), ((), ())), preferred_element_...]
  transfers between devices with their start and end apart: 9 -> 0, of which waited for: 9 -> 0; matrix products, arithmetic and copies ran while one was open for 4% -> 0% of each run, Pallas kernels for 0% -> 0%
where the time goes in v1:
time: 148 us
  Pallas kernels  143 us (97%)
  other arithmetic  2.62 us (2%)
  local copies, waits for them, and re-layouts  2.35 us (2%)
    pallas_call x1, Pallas kernels, on_device(): pl.pallas_call(kernel, out_shape=(jax.ShapeDtypeStruct((512, 128), F32),...  143 us

profile of v1, /device:TPU:1, one launch (start us, length us, event | category | flops | bytes accessed | tf_op | source)
XLA Modules:
  0.0 148.2 jit_solution(6855959191078469620)
XLA Ops:
  0.6 142.6 %backward.1 = (f32[512,128]{1,0:T(8,128)}, f32[3,32,512]{2,1,0:T(8,128)}, bf16[128,1024]{1,0:T(8,128)(2,1)}) custom-call(bf16[128,4096]{1,0:T(8,128)(2,1)} %cot_in.1, bf16[128,1024]{1,0:T(8,128)(2,1)} %feat_in.1, bf16[128,1024]{1,0:T(8,128)(2,1)} %norm_in.1, bf16[1024,512]{1,0:T(8,128)(2,1)} %preh_in.1, bf16[1024,512]{1,0:T(8,128)(2,1)} %prei_in.1, ...), custom_call_target="tpu_custom_call" | custom-call | tf_op jit(solution)/shard_map/backward/pallas_call | solution.py:454
  143.2 1.7 %broadcast_multiply_fusion = f32[512,128]{1,0:T(8,128)} fusion(f32[512,128]{1,0:T(8,128)} %get-tuple-element.8), kind=kLoop, calls=%fused_computation | loop fusion | flops 65536 | bytes 524288 | tf_op jit(solution)/shard_map/mul | solution.py:502
  144.9 0.9 broadcast_multiply_fusion.1
  145.8 0.7 slice_bitcast_fusion
  146.5 1.7 %copy.14 = bf16[128,1024]{1,0:T(8,128)(2,1)} copy(bf16[128,1024]{1,0:T(8,128)(2,1)} %get-tuple-element.23) | data formatting | bytes 524288

commit v2 on v1

--- a/solution.py
+++ b/solution.py
@@ -1,3 +1,4 @@
+import functools
 import math
 
 import jax
@@ -147,7 +148,6 @@
     def chunk_start(k):
         wait(cot.at[k, pl.ds(pl.multiple_of(mine * 128, 128), 128)], cot_l.at[k])
         gather_start(k)
-        weights_start(k)
 
     def halves_start(src, dst, size, sems, first, to):
         part = pl.ds(pl.multiple_of(c * size, size), size)
@@ -302,9 +302,12 @@
             cols = slice(part * 512, (part + 1) * 512)
             smp[i, cols, :] = dot_tn(left[:, cols], right[...]).astype(BF)
 
+    chunk_start(0)
+    weights_start(0)
     pre_start(0, preh_in, preh)
-    chunk_start(0)
     chunk_start(1)
+    weights_start(1)
+    weights_start(2)
     dhid[...] = jnp.zeros_like(dhid)
 
     @pl.loop(0, K + 2)
@@ -313,14 +316,24 @@
         def _():
             chunk_start(t + 2)
 
-        @pl.when(t == 5)
+        @pl.when(t + 3 < K)
+        def _():
+            weights_start(t + 3)
+
+        @pl.when(t == 3)
         def _():
             halves_start(w1_in, w1, 512, w1_r, 0, outer)
+
+        @pl.when(t == 6)
+        def _():
             pre_start(1, prei_in, prei)
 
-        @pl.when(t == 6)
+        @pl.when(t == 7)
         def _():
             halves_start(wd_in, wd, 256, wd_r, 1, outer)
+
+        @pl.when(t == 8)
+        def _():
             wait(rows_of(feat, mine), fn_l.at[0])
             gather_start(FEAT)
 
@@ -335,10 +348,6 @@
         @pl.when(t == 2)
         def _():
             hidden_parts()
-
-        @pl.when(t >= 4)
-        def _():
-            chunk_sum(t - 4)
 
         @pl.when(t >= 2)
         def _():
@@ -373,12 +382,16 @@
         send(encs.at[o - 1], encr.at[o - 1], ex_s.at[o - 1], ex_r.at[o - 1], device(to, y, z, c))
     wait(rows_of(norm, mine), fn_l.at[1])
     gather_start(NORM)
+    chunk_sum(0)
+    chunk_sum(1)
+    chunk_sum(2)
     gather_last(FEAT)
-    chunk_sum(K - 2)
-    chunk_sum(K - 1)
+    chunk_sum(3)
+    chunk_sum(4)
     gather_end(FEAT)
     row_product(0, feat, dpre)
     small_start(0)
+    chunk_sum(5)
     inner_parts()
     total = encp[c, x].astype(F32) + encc[x].astype(F32)
     for o in range(3):
@@ -388,6 +401,8 @@
     enc[pl.ds(pl.multiple_of(mine * 128, 128), 128), :] = own_rows
     o_enc[...] = own_rows
     gather_start(ENC)
+    chunk_sum(6)
+    chunk_sum(7)
     gather_middle(NORM)
     gather_middle(ENC)
     gather_last(ENC)
@@ -444,6 +459,14 @@
         wait(encr.at[o], ex_s.at[o])
     for i in range(3):
         small_sent(i)
+
+
+def finish(gs, small, own_rows, o_gs, o_first, o_down, o_up, o_enc, *, factor):
+    o_gs[...] = gs[...] * factor
+    o_first[...] = small[0] * factor
+    o_down[...] = jnp.transpose(small[1] * factor)
+    o_up[...] = small[2] * factor
+    o_enc[...] = own_rows[...]
 
 
 def on_device(cotangent, features, normed, pre_hidden, pre_inner, w_first, w_second, w_down):
@@ -499,8 +522,17 @@
         ),
         name="backward",
     )(cotangent, features, normed, pre_hidden, pre_inner, w_first, w_second, w_down)
-    gs, small = gs * factor, small * factor
-    return (gs, small[0], small[1].T, small[2], own_rows)
+    return pl.pallas_call(
+        functools.partial(finish, factor=factor),
+        out_shape=(
+            jax.ShapeDtypeStruct((512, 128), F32),
+            jax.ShapeDtypeStruct((32, 512), F32),
+            jax.ShapeDtypeStruct((512, 32), F32),
+            jax.ShapeDtypeStruct((32, 512), F32),
+            jax.ShapeDtypeStruct((128, 1024), BF),
+        ),
+        name="finish",
+    )(gs, small, own_rows)
 
 
 def solution(mesh):

time: 148 us -> 134 us (0.905)
  Pallas kernels: 143 us -> 132 us
  other arithmetic: 2.62 us -> 0 us
    pallas_call x1, Pallas kernels: 143 us -> 130 us  [on_device(): pl.pallas_call(kernel, out_shape=(jax.ShapeDtypeStruct((512, 128), F32),...]
    mul x2 -> x0, other arithmetic: 2.62 us -> none  [on_device(): gs, small = (gs * factor, small * factor)]
    pallas_call x0 -> x1, Pallas kernels: none -> 2.08 us  [on_device(): pl.pallas_call(functools.partial(finish, factor=factor), out_shape=(jax.S...]
    pallas_call x0 -> x1, local copies, waits for them, and re-layouts: none -> 1.69 us  [on_device(): pl.pallas_call(functools.partial(finish, factor=factor), out_shape=(jax.S...]
    unnamed x1 -> x0, local copies, waits for them, and re-layouts: 1.67 us -> none
where the time goes in v2:
time: 134 us
  Pallas kernels  132 us (99%)
  local copies, waits for them, and re-layouts  1.69 us (1%)
    pallas_call x1, Pallas kernels, on_device(): pl.pallas_call(kernel, out_shape=(jax.ShapeDtypeStruct((512, 128), F32),...  130 us

profile of v2, /device:TPU:1, one launch (start us, length us, event | category | flops | bytes accessed | tf_op | source)
XLA Modules:
  0.0 134.2 jit_solution(11612646121722928480)
XLA Ops:
  0.6 129.8 %backward.1 = (f32[512,128]{1,0:T(8,128)}, f32[3,32,512]{2,1,0:T(8,128)}, bf16[128,1024]{1,0:T(8,128)(2,1)}) custom-call(bf16[128,4096]{1,0:T(8,128)(2,1)} %cot_in.1, bf16[128,1024]{1,0:T(8,128)(2,1)} %feat_in.1, bf16[128,1024]{1,0:T(8,128)(2,1)} %norm_in.1, bf16[1024,512]{1,0:T(8,128)(2,1)} %preh_in.1, bf16[1024,512]{1,0:T(8,128)(2,1)} %prei_in.1, ...), custom_call_target="tpu_custom_call" | custom-call | tf_op jit(solution)/shard_map/backward/pallas_call | solution.py:477
  130.4 2.1 %finish.1 = (f32[512,128]{1,0:T(8,128)}, f32[32,512]{1,0:T(8,128)}, f32[512,32]{1,0:T(8,128)}, f32[32,512]{1,0:T(8,128)}, bf16[128,1024]{1,0:T(8,128)(2,1)}) custom-call(f32[512,128]{1,0:T(8,128)} %get-tuple-element.8.gs, f32[3,32,512]{2,1,0:T(8,128)} %get-tuple-element.9.small, bf16[128,1024]{1,0:T(8,128)(2,1)} %get-tuple-element.10.own_rows), custom_call_target="tpu_custom_call" | custom-call | tf_op jit(solution)/shard_map/finish/pallas_call | solution.py:525
  132.5 1.7 %copy.13 = f32[512,32]{0,1:T(8,128)} copy(f32[512,32]{1,0:T(8,128)} %get-tuple-element.13) | data formatting | bytes 131072 | tf_op jit(solution)/shard_map/finish/pallas_call | solution.py:525

commit v3 on v2

--- a/solution.py
+++ b/solution.py
@@ -47,11 +47,11 @@
     o_gs, o_small, o_enc,
     cot, w2, w1, wd, preh, prei, feat, norm, hact_t, slope, dhid, dpre,
     encp, encc, encs, encr, enc, iact, dinner,
-    gsp, gsr, gsy, gsz, smp, smr, smy, smz,
+    gsp, gsr, gsy, gsz, smp, smr, smy, smz, sdp, sdr, sdy, sdz,
     ag_s, ag_r, cot_l, w2_l, fn_l,
     w2_s, w2_r, w_s, w1_r, wd_r, pre_s, pre_r,
     ec_s, ec_r, ex_s, ex_r,
-    gy_s, gy_r, gz_s, gz_r, sy_s, sy_r, sz_s, sz_r,
+    gy_s, gy_r, gz_s, gz_r, sy_s, sy_r, sz_s, sz_r, dz_s, dz_r, dy_s, dy_r,
 ):
     dp, tensor = lax.axis_index("dp"), lax.axis_index("tensor")
     y, zh, c = dp // 8, lax.rem(dp // 2, 4), lax.rem(dp, 2)
@@ -90,7 +90,7 @@
 
     barrier = pltpu.get_barrier_semaphore()
     friends = [right, left, device(x2, y, z, c), other]
-    friends += [device(x, lax.rem(y + o, NY), z, c) for o in (1, 2, 3)]
+    friends += [device(x, lax.rem(y + o, NY), z, core) for o in (1, 2, 3) for core in (c, 1 - c)]
     friends += [device(x, y, lax.rem(z + o, NZ), core) for o in range(1, NZ) for core in (0, 1)]
     for friend in friends:
         pl.semaphore_signal(barrier, inc=1, device_id=friend, device_id_type=MESH)
@@ -212,6 +212,7 @@
             rows = pl.ds(pl.multiple_of(r * 512, 512), 512)
             dhid[rows, :] += dot_nt(cot[k, rows, :], w2[c, k])
 
+    def chunk_grad(k):
         for half in range(2):
             term = dot_nn(hact_t[...], cot[k, :, half * 256:(half + 1) * 256])
             gsp[k, 2 * half] = term[:, :128].astype(BF)
@@ -245,50 +246,53 @@
         def _():
             wait(gsy.at[k], gz_s.at[k])
 
-    def small_start(i):
-        for o in (1, 2, 3):
-            to = lax.rem(y + o, NY)
-            send(
-                smp.at[i, pl.ds(pl.multiple_of(to * 256, 256), 256)], smr.at[i, o - 1],
-                sy_s.at[i, o - 1], sy_r.at[i, o - 1], device(x, to, z, c),
-            )
+    def width(i):
+        return pl.ds(0, 512 if i == 0 else 384)
+
+    def small_send(i, to):
+        o = lax.rem(to - y + NY, NY)
+        send(
+            smp.at[i, pl.ds(pl.multiple_of(to * 256, 256), 256), width(i)], smr.at[i, o - 1, :, width(i)],
+            sy_s.at[i, o - 1], sy_r.at[i, o - 1], device(x, to, z, c),
+        )
 
     def small_piece(i, hi, core):
-        return smy.at[i, pl.ds(hi * 64 + core * 32, 32)]
+        return smy.at[i, pl.ds(hi * 64 + core * 32, 32), width(i)]
 
     def small_sum(i):
+        total = smp[i, pl.ds(pl.multiple_of(y * 256, 256), 256), width(i)].astype(F32)
         for o in range(3):
-            wait(smr.at[i, o], sy_r.at[i, o])
-        total = smp[i, pl.ds(pl.multiple_of(y * 256, 256), 256), :].astype(F32)
-        for o in range(3):
-            total = total + smr[i, o].astype(F32)
-        smy[i] = total.astype(BF)
+            wait(smr.at[i, o, :, width(i)], sy_r.at[i, o])
+            total = total + smr[i, o, :, width(i)].astype(F32)
+        smy[i, :, width(i)] = total.astype(BF)
         for hi in range(4):
             for core in range(2):
                 to_z = 2 * hi + c
                 own = jnp.logical_and(to_z == z, core == c)
+                to = smz.at[i, z, :, width(i)]
 
                 @pl.when(own)
                 def _():
-                    pltpu.make_async_copy(small_piece(i, hi, core), smz.at[i, z], sz_r.at[i, z]).start()
+                    pltpu.make_async_copy(small_piece(i, hi, core), to, sz_r.at[i, z]).start()
 
                 @pl.when(jnp.logical_not(own))
                 def _():
                     send(
-                        small_piece(i, hi, core), smz.at[i, z],
+                        small_piece(i, hi, core), to,
                         sz_s.at[i, hi, core], sz_r.at[i, z], device(x, y, to_z, core),
                     )
 
     def small_end(i):
-        total = jnp.zeros((32, 512), F32)
+        total = None
         for source in range(NZ):
-            wait(smz.at[i, source], sz_r.at[i, source])
-            total = total + smz[i, source].astype(F32)
-        o_small[i] = total
+            wait(smz.at[i, source, :, width(i)], sz_r.at[i, source])
+            term = smz[i, source, :, width(i)].astype(F32)
+            total = term if total is None else total + term
+        o_small[i, :, width(i)] = total
 
     def small_sent(i):
         for o in range(3):
-            wait(smr.at[i, o], sy_s.at[i, o])
+            wait(smr.at[i, o, :, width(i)], sy_s.at[i, o])
         for hi in range(4):
             for core in range(2):
                 own = jnp.logical_and(2 * hi + c == z, core == c)
@@ -297,10 +301,74 @@
                 def _():
                     wait(small_piece(i, hi, core), sz_s.at[i, hi, core])
 
+    def side_start(j):
+        for hi in range(4):
+            to_z = 2 * hi + c
+
+            @pl.when(to_z != z)
+            def _():
+                send(sdp.at[j, hi], sdr.at[j, z], dz_s.at[j, hi], dz_r.at[j, z], device(x, y, to_z, c))
+
+    def side_sum(j):
+        @pl.when(home)
+        def _():
+            sdr[j, z] = sdp[j, zh]
+            total = jnp.zeros((256, 128), F32)
+            for source in range(NZ):
+                @pl.when(source != z)
+                def _():
+                    wait(sdr.at[j, source], dz_r.at[j, source])
+
+            for source in range(NZ):
+                total = total + sdr[j, source].astype(F32)
+            sdy[j] = total.astype(BF)
+            for o in range(NY):
+                to = lax.rem(y + o, NY)
+                for flip in range(2):
+                    core = c if flip == 0 else 1 - c
+                    piece = sdy.at[j, pl.ds(pl.multiple_of(to * 64 + core * 32, 32), 32)]
+                    if o == 0 and flip == 0:
+                        pltpu.make_async_copy(piece, sdz.at[j, y], dy_r.at[j, y]).start()
+                    else:
+                        send(piece, sdz.at[j, y], dy_s.at[j, o, flip], dy_r.at[j, y], device(x, to, z, core))
+
+    def side_end(j):
+        total = None
+        for source in range(NY):
+            wait(sdz.at[j, source], dy_r.at[j, source])
+            term = sdz[j, source].astype(F32)
+            total = term if total is None else total + term
+        o_small[j + 1, :, 384:] = total
+
+    def side_sent(j):
+        for hi in range(4):
+            @pl.when(2 * hi + c != z)
+            def _():
+                wait(sdp.at[j, hi], dz_s.at[j, hi])
+
+        @pl.when(home)
+        def _():
+            for o in range(NY):
+                for flip in range(2):
+                    if o + flip > 0:
+                        wait(sdz.at[j, 0], dy_s.at[j, o, flip])
+
+    def row_store(i, part, term):
+        smp[i, part * 512:(part + 1) * 512, :] = term.astype(BF)
+        if i > 0:
+            for two in range(2):
+                for hi in range(4):
+                    at = (2 * part + two) * 64
+                    sdp[i - 1, hi, at:at + 64, :] = term[two * 256 + hi * 64:two * 256 + hi * 64 + 64, 384:].astype(BF)
+
     def row_product(i, left, right):
         for part in range(2):
             cols = slice(part * 512, (part + 1) * 512)
-            smp[i, cols, :] = dot_tn(left[:, cols], right[...]).astype(BF)
+            row_store(i, part, dot_tn(left[:, cols], right[...]))
+            for to in (2 * part, 2 * part + 1):
+                @pl.when(y != to)
+                def _():
+                    small_send(i, to)
 
     chunk_start(0)
     weights_start(0)
@@ -312,10 +380,6 @@
 
     @pl.loop(0, K + 2)
     def _(t):
-        @pl.when(t + 2 < K)
-        def _():
-            chunk_start(t + 2)
-
         @pl.when(t + 3 < K)
         def _():
             weights_start(t + 3)
@@ -340,6 +404,10 @@
         @pl.when(t < K)
         def _():
             gather_middle(t)
+
+        @pl.when(t + 2 < K)
+        def _():
+            chunk_start(t + 2)
 
         @pl.when(jnp.logical_and(t >= 1, t <= K))
         def _():
@@ -355,11 +423,16 @@
             weights_end(t - 2)
             chunk_work(t - 2)
 
-    @pl.loop(0, 4)
-    def _(r):
-        rows = pl.ds(pl.multiple_of(r * 256, 256), 256)
-        dpre[rows, :] = (dhid[rows, :] * slope[rows, :]).astype(BF)
-
+        @pl.when(jnp.logical_and(t >= 2, t <= K))
+        def _():
+            chunk_grad(t - 2)
+
+    def slopes(core):
+        for part in range(2):
+            rows = pl.ds(pl.multiple_of(core * 512 + part * 256, 256), 256)
+            dpre[rows, :] = (dhid[rows, :] * slope[rows, :]).astype(BF)
+
+    slopes(1 - c)
     halves_end(w1, 512, w1_r)
 
     def partials(core):
@@ -372,8 +445,9 @@
     partials(1 - c)
     for at in range(4):
         send(encp.at[1 - c, at], encc.at[at], ec_s.at[at], ec_r.at[at], other)
+    slopes(c)
+    partials(c)
     gather_middle(FEAT)
-    partials(c)
     for at in range(4):
         wait(encc.at[at], ec_r.at[at])
     for o in (2, 1, 3):
@@ -382,6 +456,7 @@
         send(encs.at[o - 1], encr.at[o - 1], ex_s.at[o - 1], ex_r.at[o - 1], device(to, y, z, c))
     wait(rows_of(norm, mine), fn_l.at[1])
     gather_start(NORM)
+    chunk_grad(K - 1)
     chunk_sum(0)
     chunk_sum(1)
     chunk_sum(2)
@@ -390,7 +465,6 @@
     chunk_sum(4)
     gather_end(FEAT)
     row_product(0, feat, dpre)
-    small_start(0)
     chunk_sum(5)
     inner_parts()
     total = encp[c, x].astype(F32) + encc[x].astype(F32)
@@ -410,7 +484,7 @@
     small_sum(0)
     gather_end(ENC)
     row_product(1, enc, iact)
-    small_start(1)
+    side_start(0)
     halves_end(wd, 256, wd_r)
 
     @pl.loop(0, 4)
@@ -420,7 +494,7 @@
 
     gather_end(NORM)
     row_product(2, norm, dinner)
-    small_start(2)
+    side_start(1)
 
     total = jnp.zeros((512, 128), F32)
     for source in range(NZ):
@@ -428,9 +502,13 @@
         total = total + gsz[source].astype(F32)
     o_gs[...] = total
     small_end(0)
+    side_sum(0)
     small_sum(1)
+    side_sum(1)
     small_sum(2)
     small_end(1)
+    side_end(0)
+    side_end(1)
     small_end(2)
 
     @pl.loop(0, K)
@@ -459,12 +537,14 @@
         wait(encr.at[o], ex_s.at[o])
     for i in range(3):
         small_sent(i)
+    for j in range(2):
+        side_sent(j)
 
 
 def finish(gs, small, own_rows, o_gs, o_first, o_down, o_up, o_enc, *, factor):
     o_gs[...] = gs[...] * factor
     o_first[...] = small[0] * factor
-    o_down[...] = jnp.transpose(small[1] * factor)
+    o_down[...] = small[1] * factor
     o_up[...] = small[2] * factor
     o_enc[...] = own_rows[...]
 
@@ -511,28 +591,34 @@
             vmem((3, 3, 256, 512), BF),
             vmem((3, 256, 512), BF),
             vmem((3, NZ, 32, 512), BF),
+            vmem((2, 4, 256, 128), BF),
+            vmem((2, NZ, 256, 128), BF),
+            vmem((2, 256, 128), BF),
+            vmem((2, NY, 32, 128), BF),
             dma((K + 3, 8)), dma((K + 3, 8)), dma((K,)), dma((K,)), dma((2,)),
             dma((K, 2)), dma((K, 4)), dma((2,)), dma((2,)), dma((2,)), dma((2, 2)), dma((2, 2)),
             dma((4,)), dma((4,)), dma((3,)), dma((3,)),
             dma((K, 3)), dma((K, 3)), dma((K,)), dma((NZ,)),
             dma((3, 3)), dma((3, 3)), dma((3, 4, 2)), dma((3, NZ)),
+            dma((2, 4)), dma((2, NZ)), dma((2, NY, 2)), dma((2, NY)),
         ],
         compiler_params=pltpu.CompilerParams(
             collective_id=0, has_side_effects=True, vmem_limit_bytes=63 * 2**20
         ),
         name="backward",
     )(cotangent, features, normed, pre_hidden, pre_inner, w_first, w_second, w_down)
-    return pl.pallas_call(
+    grad_second, first, down_rows, grad_up, enc_rows = pl.pallas_call(
         functools.partial(finish, factor=factor),
         out_shape=(
             jax.ShapeDtypeStruct((512, 128), F32),
             jax.ShapeDtypeStruct((32, 512), F32),
-            jax.ShapeDtypeStruct((512, 32), F32),
+            jax.ShapeDtypeStruct((32, 512), F32),
             jax.ShapeDtypeStruct((32, 512), F32),
             jax.ShapeDtypeStruct((128, 1024), BF),
         ),
         name="finish",
     )(gs, small, own_rows)
+    return (grad_second, first, down_rows.T, grad_up, enc_rows)
 
 
 def solution(mesh):

time: 134 us -> 123 us (0.918)
  Pallas kernels: 132 us -> 123 us
  local copies, waits for them, and re-layouts: 1.69 us -> 0 us
    pallas_call x1, Pallas kernels: 130 us -> 121 us  [on_device(): pl.pallas_call(kernel, out_shape=(jax.ShapeDtypeStruct((512, 128), F32),...]
    pallas_call x1 -> x0, local copies, waits for them, and re-layouts: 1.69 us -> none  [on_device(): pl.pallas_call(functools.partial(finish, factor=factor), out_shape=(jax.S...]
where the time goes in v3:
time: 123 us
  Pallas kernels  123 us (100%)
    pallas_call x1, Pallas kernels, on_device(): pl.pallas_call(kernel, out_shape=(jax.ShapeDtypeStruct((512, 128), F32),...  121 us

profile of v3, /device:TPU:1, one launch (start us, length us, event | category | flops | bytes accessed | tf_op | source)
XLA Modules:
  0.0 123.3 jit_solution(7445713525809017567)
XLA Ops:
  0.6 120.7 %backward.1 = (f32[512,128]{1,0:T(8,128)}, f32[3,32,512]{2,1,0:T(8,128)}, bf16[128,1024]{1,0:T(8,128)(2,1)}) custom-call(bf16[128,4096]{1,0:T(8,128)(2,1)} %cot_in.1, bf16[128,1024]{1,0:T(8,128)(2,1)} %feat_in.1, bf16[128,1024]{1,0:T(8,128)(2,1)} %norm_in.1, bf16[1024,512]{1,0:T(8,128)(2,1)} %preh_in.1, bf16[1024,512]{1,0:T(8,128)(2,1)} %prei_in.1, ...), custom_call_target="tpu_custom_call" | custom-call | tf_op jit(solution)/shard_map/backward/pallas_call | solution.py:557
  121.3 2.0 %finish.1 = (f32[512,128]{1,0:T(8,128)}, f32[32,512]{1,0:T(8,128)}, f32[32,512]{1,0:T(8,128)}, f32[32,512]{1,0:T(8,128)}, bf16[128,1024]{1,0:T(8,128)(2,1)}) custom-call(f32[512,128]{1,0:T(8,128)} %get-tuple-element.13.gs, f32[3,32,512]{2,1,0:T(8,128)} %get-tuple-element.14.small, bf16[128,1024]{1,0:T(8,128)(2,1)} %get-tuple-element.15.own_rows), custom_call_target="tpu_custom_call" | custom-call | tf_op jit(solution)/shard_map/finish/pallas_call | solution.py:610

commit v4 on v3

--- a/solution.py
+++ b/solution.py
@@ -101,7 +101,6 @@
         own = rows_of(buf, mine)
         send(own, own, ag_s.at[item, 0], ag_r.at[item, 0], right)
         send(own, own, ag_s.at[item, 1], ag_r.at[item, 1], left)
-        send(own, own, ag_s.at[item, 2], ag_r.at[item, 4], other)
 
     def gather_middle(item):
         buf = view(item)
@@ -114,6 +113,8 @@
         half = rows_of(buf, c * 4 + xp, 64, 64)
         send(half, half, ag_s.at[item, 5], ag_r.at[item, 3], left)
         send(from_right, from_right, ag_s.at[item, 6], ag_r.at[item, 6], other)
+        own = rows_of(buf, mine)
+        send(own, own, ag_s.at[item, 2], ag_r.at[item, 4], other)
 
     def gather_last(item):
         buf = view(item)

time: 123 us -> 123 us (level)
  no operation moved by 1% of the time
where the time goes in v4:
time: 123 us
  Pallas kernels  123 us (100%)
    pallas_call x1, Pallas kernels, on_device(): pl.pallas_call(kernel, out_shape=(jax.ShapeDtypeStruct((512, 128), F32),...  121 us

profile of v4, /device:TPU:1, one launch (start us, length us, event | category | flops | bytes accessed | tf_op | source)
XLA Modules:
  0.0 123.3 jit_solution(3012624664336383735)
XLA Ops:
  0.6 120.6 %backward.1 = (f32[512,128]{1,0:T(8,128)}, f32[3,32,512]{2,1,0:T(8,128)}, bf16[128,1024]{1,0:T(8,128)(2,1)}) custom-call(bf16[128,4096]{1,0:T(8,128)(2,1)} %cot_in.1, bf16[128,1024]{1,0:T(8,128)(2,1)} %feat_in.1, bf16[128,1024]{1,0:T(8,128)(2,1)} %norm_in.1, bf16[1024,512]{1,0:T(8,128)(2,1)} %preh_in.1, bf16[1024,512]{1,0:T(8,128)(2,1)} %prei_in.1, ...), custom_call_target="tpu_custom_call" | custom-call | tf_op jit(solution)/shard_map/backward/pallas_call | solution.py:558
  121.3 2.0 %finish.1 = (f32[512,128]{1,0:T(8,128)}, f32[32,512]{1,0:T(8,128)}, f32[32,512]{1,0:T(8,128)}, f32[32,512]{1,0:T(8,128)}, bf16[128,1024]{1,0:T(8,128)(2,1)}) custom-call(f32[512,128]{1,0:T(8,128)} %get-tuple-element.13.gs, f32[3,32,512]{2,1,0:T(8,128)} %get-tuple-element.14.small, bf16[128,1024]{1,0:T(8,128)(2,1)} %get-tuple-element.15.own_rows), custom_call_target="tpu_custom_call" | custom-call | tf_op jit(solution)/shard_map/finish/pallas_call | solution.py:611
